TPU v7x, 128 devices: a whole 4x4x4 slice. The times are simulated.
128 devices in a mesh: group: 16 (over x, z), owner: 8 (over y, core).
Axes of the slice: x: 4, y: 4, z: 4, core: 2. Of those that a mesh axis runs over, the one named last changes fastest.
Arguments:
- embeddings: bfloat16 [131072, 1024], P(('group', 'owner')), may hold values from -2 to 2
- home_pairs: int32 [16, 8, 5, 64, 2], P('group', 'owner'), may hold values from 0 to 7, as said below
- home_count: int32 [16, 8, 5], P('group', 'owner'), may hold values from 0 to 20
- surplus_pairs: int32 [16, 8, 16, 3], P('group', 'owner'), may hold values from 0 to 7, as said below
Outputs:
- centered: bfloat16 [131072, 1024], P(('group', 'owner'))
- log_density: float32 [131072], P(('group', 'owner'))
Inputs may be any that keep to these rules, and one draw needn't show every extreme that they name: `home_pairs`: for owner o of group g and distance s, the first home_count[g, o, s] slots hold distinct pairs (a, b) of block a of owner o and block b of owner (o + s) mod 8 that lie in one cluster; at distance 0 a <= b and every pair (a, a) is listed; at twice s equal to 8 only owners below 4 list pairs; later slots are ignored. `surplus_pairs`: A live entry (a, b, 1) names two blocks of the same owner in one cluster with a < b; no pair is live twice or also listed in home_pairs; dead entries are ignored.
All inputs are finite; a program needn't handle non-finite values.
Results may differ from a plain program's by a relative error of at most 0.0057.
Values may be sent and summed in bfloat16 or wider, within the bound.
No kernel may reach another device: no remote copies, remote signals or barrier semaphores. Data moves between devices by JAX's collectives and lax.ppermute only.
A program may use at most 128 MiB of HBM per device.

v0:
```python
import functools

import jax
import jax.numpy as jnp
from jax import lax
from jax.experimental import pallas as pl
from jax.experimental.pallas import tpu as pltpu
from jax.sharding import PartitionSpec as P

BLOCK = 128
BPD = 8
CHIPS = 4
OWNERS = 8
BLOCKS = OWNERS * BPD
ON_CHIP = 2 * BPD
sharpness = 4.0
epsilon = 1e-06
SIZES = ((3, 3), (4, 4), (8, 8))
MOST = 20
ENTRY = MOST + 1

STRIDE = 32
F_COUNT, D_COUNT, LOAD, FIRST, NEED, TOUCHED, FAR, F_LIST, D_LIST = 0, 8, 16, 24, 32, 96, 161, 256, 512
PLAN = 768
TASKS, TASK, PLACE = 0, 16, 1040
PLACES = 1152


def loop(count, body):
    def step(i, carry):
        body(i)
        return carry

    lax.fori_loop(0, count, step, 0)


def along_chips(x, hops):
    route = [(o, ((o // 2 + hops) % CHIPS) * 2 + o % 2) for o in range(OWNERS)]
    return lax.ppermute(x, "owner", route)


def to_sibling(x):
    return lax.ppermute(x, "owner", [(o, o ^ 1) for o in range(OWNERS)])


def normalize_kernel(x_ref, u_ref):
    wide = x_ref[...].astype(jnp.float32)
    mean = jnp.mean(wide * wide, axis=-1, keepdims=True)
    u_ref[...] = (wide * lax.rsqrt(mean + epsilon)).astype(jnp.bfloat16)


def rows_of(block):
    return pl.ds(pl.multiple_of(block * BLOCK, BLOCK), BLOCK)


def kernel_values(p, q):
    dots = lax.dot_general(p, q, (((1,), (1,)), ((), ())), preferred_element_type=jnp.float32)
    return jnp.exp(sharpness * (dots * (1.0 / q.shape[1]) - 1.0))


def add_terms(u_ref, q_ref, acc_ref, kacc_ref, mine, other):
    q = q_ref[rows_of(other), :]
    kernel = kernel_values(u_ref[rows_of(mine), :], q)
    kacc_ref[rows_of(mine), :] += kernel
    acc_ref[rows_of(mine), :] += jnp.dot(
        kernel.astype(jnp.bfloat16), q, preferred_element_type=jnp.float32
    )


def plan_kernel(pos_ref, tab_ref, plan_ref, class_ref):
    me = pos_ref[0]
    for i in range(8):
        plan_ref[LOAD + i] = 0
        plan_ref[F_COUNT + i] = 0
        plan_ref[D_COUNT + i] = 0
    for i in range(BLOCKS):
        plan_ref[NEED + i] = 0

    def of_owner(o, touched):
        row = o ^ me
        for s in range(1, 5):
            q = (o + s) & 7
            to_q, to_o = lax.shift_left(1, q >> 1), lax.shift_left(1, o >> 1)

            def of_pair(t, touched):
                pair = tab_ref[row, s * ENTRY + 1 + t]
                for block, chip in ((o * BPD + (pair >> 3), to_q), (q * BPD + (pair & 7), to_o)):
                    before = plan_ref[NEED + block]
                    plan_ref[NEED + block] = before | chip
                    plan_ref[TOUCHED + touched] = block
                    touched = touched + (before == 0).astype(jnp.int32)
                return touched

            touched = lax.fori_loop(0, tab_ref[row, s * ENTRY], of_pair, touched)
        return touched

    touched = lax.fori_loop(0, OWNERS, of_owner, 0)

    def needs(block):
        mask, chip = plan_ref[NEED + block], block >> 4
        bit = lambda hop: lax.shift_right_logical(mask, (chip + hop) & 3) & 1
        return chip, bit(1), bit(3), bit(2)

    def append(count, table, at, block, wanted):
        held = plan_ref[count + at]
        plan_ref[table + at * STRIDE + held] = block
        plan_ref[count + at] = held + wanted

    def one_hop(i, fars):
        block = plan_ref[TOUCHED + i]
        chip, up, down, far = needs(block)
        at = 2 * chip
        plan_ref[LOAD + at] = plan_ref[LOAD + at] + up
        plan_ref[LOAD + at + 1] = plan_ref[LOAD + at + 1] + down
        append(D_COUNT, D_LIST, at, block, up & (1 - far))
        append(D_COUNT, D_LIST, at + 1, block, down & (1 - far))
        plan_ref[FAR + fars] = block
        return fars + far

    fars = lax.fori_loop(0, touched, one_hop, 0)

    @functools.partial(loop, fars)
    def _(i):
        block = plan_ref[FAR + i]
        chip, up, down, _ = needs(block)
        costs, loads = [], []
        for way, near, hop in ((0, up, 1), (1, down, 3)):
            at, after = 2 * chip + way, 2 * ((chip + hop) & 3) + way
            here, there = plan_ref[LOAD + at] + 1 - near, plan_ref[LOAD + after] + 1
            most = jnp.maximum(jnp.maximum(here, there), 2 * plan_ref[F_COUNT + at] + 2)
            costs.append(most * 64 + here + there + 32 * (1 - near))
            loads.append((at, after, here, there))
        goes_down = costs[0] > costs[1]
        at, after, here, there = (jnp.where(goes_down, b, a) for a, b in zip(*loads))
        plan_ref[LOAD + at] = here
        plan_ref[LOAD + after] = there
        append(F_COUNT, F_LIST, at, block, 1)
        append(D_COUNT, D_LIST, at ^ 1, block, jnp.where(goes_down, up, down))

    twice = [plan_ref[F_COUNT + i] for i in range(8)]
    once = [plan_ref[D_COUNT + i] for i in range(8)]
    longest = functools.reduce(jnp.maximum, twice)
    second_needs = {}
    for size in sorted({size for size, _ in SIZES}):
        needs = []
        for i in range(8):
            before = (i + (6 if i % 2 == 0 else 2)) % 8
            needs.append(twice[before] + jnp.maximum(twice[i] + once[i] - 2 * size, 0))
        second_needs[size] = functools.reduce(jnp.maximum, needs)
    chosen, first_size = len(SIZES) - 1, 2 * SIZES[-1][0]
    for k in range(len(SIZES) - 2, -1, -1):
        first, second = SIZES[k]
        fits = (longest <= 2 * first) & (second_needs[first] <= 2 * second)
        chosen = jnp.where(fits, k, chosen)
        first_size = jnp.where(fits, 2 * first, first_size)
    class_ref[0] = chosen
    plan_ref[FIRST] = first_size


def places_kernel(pos_ref, tab_ref, plan_ref, out_ref):
    me = pos_ref[0]
    y, core = me >> 1, me & 1
    first_size = plan_ref[FIRST]
    for i in range(16):
        out_ref[TASKS + i] = 0

    def put(block, stage, way, position):
        other = (position & 1) ^ core
        out_ref[PLACE + block] = stage * 65536 + (way * 2 + other) * 256 + (position >> 1)

    for way in (0, 1):
        near = 2 * ((y + (3 if way == 0 else 1)) & 3) + way
        far = 2 * ((y + 2) & 3) + way
        twice, passing = plan_ref[F_COUNT + near], plan_ref[F_COUNT + far]

        @functools.partial(loop, twice)
        def _(i):
            put(plan_ref[F_LIST + near * STRIDE + i], 0, way, i)

        @functools.partial(loop, plan_ref[D_COUNT + near])
        def _(i):
            late = (twice + i >= first_size).astype(jnp.int32)
            put(plan_ref[D_LIST + near * STRIDE + i], late, way, twice + i + late * (passing - first_size))

        @functools.partial(loop, passing)
        def _(i):
            put(plan_ref[F_LIST + far * STRIDE + i], 1, way, i)

    def add_task(own, block):
        place = out_ref[PLACE + block]
        row = (place >> 16) * BPD + own
        count = out_ref[TASKS + row]
        out_ref[TASK + row * 64 + count] = place & 65535
        out_ref[TASKS + row] = count + 1

    for s in range(1, 5):
        above, below = (me + s) & 7, (me - s) & 7

        @pl.when((above >> 1) != y)
        def _():
            @functools.partial(loop, tab_ref[0, s * ENTRY])
            def _(t):
                pair = tab_ref[0, s * ENTRY + 1 + t]
                add_task(pair >> 3, above * BPD + (pair & 7))

        @pl.when((below >> 1) != y)
        def _():
            row = below ^ me

            @functools.partial(loop, tab_ref[row, s * ENTRY])
            def _(t):
                pair = tab_ref[row, s * ENTRY + 1 + t]
                add_task(pair & 7, below * BPD + (pair >> 3))


def start_from(id_, core, unit_ref, sib_ref, dst, sem):
    here = rows_of(id_ & 7)
    mine = ((id_ >> 3) & 1) == core

    @pl.when(mine)
    def _():
        pltpu.make_async_copy(unit_ref.at[here, :], dst, sem).start()

    @pl.when(jnp.logical_not(mine))
    def _():
        pltpu.make_async_copy(sib_ref.at[here, :], dst, sem).start()


def listed(plan_ref, row, i, chip):
    twice, once = plan_ref[F_COUNT + row], plan_ref[D_COUNT + row]
    from_f = plan_ref[F_LIST + row * STRIDE + jnp.clip(i, 0, 15)]
    from_d = plan_ref[D_LIST + row * STRIDE + jnp.clip(i - twice, 0, 15)]
    found = jnp.where(i < twice, from_f, from_d)
    return jnp.where(i < twice + once, found, chip * ON_CHIP)


def first_pack_kernel(size, pos_ref, plan_ref, unit_ref, sib_ref, up_ref, down_ref, sems):
    y, core = pos_ref[0] >> 1, pos_ref[0] & 1
    slots = [(way, j, out) for way, out in ((0, up_ref), (1, down_ref)) for j in range(size)]
    for n, (way, j, out) in enumerate(slots):
        block = listed(plan_ref, 2 * y + way, 2 * j + core, y)
        start_from(block, core, unit_ref, sib_ref, out.at[j * BLOCK : (j + 1) * BLOCK, :], sems.at[n])
    for n, (way, j, out) in enumerate(slots):
        pltpu.make_async_copy(
            unit_ref.at[0:BLOCK, :], out.at[j * BLOCK : (j + 1) * BLOCK, :], sems.at[n]
        ).wait()


def second_pack_kernel(
    first, size, pos_ref, plan_ref, unit_ref, sib_ref, got_up, got_down, up_ref, down_ref, sems
):
    y, core = pos_ref[0] >> 1, pos_ref[0] & 1
    slots = [
        (way, j, out, got)
        for way, out, got in ((0, up_ref, got_up), (1, down_ref, got_down))
        for j in range(size)
    ]
    for n, (way, j, out, got) in enumerate(slots):
        dst = out.at[j * BLOCK : (j + 1) * BLOCK, :]
        position = 2 * j + core
        passing = plan_ref[F_COUNT + 2 * ((y + (3 if way == 0 else 1)) & 3) + way]
        passes = (position < passing) if j < first else (position < 0)
        if j < first:

            @pl.when(passes)
            def _():
                pltpu.make_async_copy(got.at[j * BLOCK : (j + 1) * BLOCK, :], dst, sems.at[n]).start()

        @pl.when(jnp.logical_not(passes))
        def _():
            block = listed(plan_ref, 2 * y + way, position - passing + 2 * first, y)
            start_from(block, core, unit_ref, sib_ref, dst, sems.at[n])

    for n, (way, j, out, got) in enumerate(slots):
        pltpu.make_async_copy(
            unit_ref.at[0:BLOCK, :], out.at[j * BLOCK : (j + 1) * BLOCK, :], sems.at[n]
        ).wait()


def own_kernel(pos_ref, tab_ref, surplus_ref, u_ref, sib_ref, acc_ref, kacc_ref, live_ref):
    core = pos_ref[0] & 1

    @functools.partial(loop, BPD * BPD)
    def _(i):
        live_ref[i] = 0.0

    def mark(a, b):
        live_ref[a * BPD + b] = 1.0
        live_ref[b * BPD + a] = 1.0

    @functools.partial(loop, tab_ref[0, 0])
    def _(t):
        pair = tab_ref[0, 1 + t]
        mark(pair >> 3, pair & 7)

    @functools.partial(loop, surplus_ref.shape[0])
    def _(t):
        @pl.when(surplus_ref[t, 2] == 1)
        def _():
            mark(surplus_ref[t, 0], surplus_ref[t, 1])

    step = 2

    @functools.partial(loop, BPD // step)
    def _(part):
        here = pl.ds(pl.multiple_of(part * step * BLOCK, step * BLOCK), step * BLOCK)
        kernel = kernel_values(u_ref[here, :], u_ref[...])
        rows = []
        for i in range(step):
            parts = [
                kernel[i * BLOCK : (i + 1) * BLOCK, j * BLOCK : (j + 1) * BLOCK]
                * live_ref[(part * step + i) * BPD + j]
                for j in range(BPD)
            ]
            kacc_ref[rows_of(part * step + i), :] = sum(parts)
            rows.append(jnp.concatenate(parts, axis=1).astype(jnp.bfloat16))
        acc_ref[here, :] = jnp.dot(
            jnp.concatenate(rows, axis=0), u_ref[...], preferred_element_type=jnp.float32
        )

    @functools.partial(loop, tab_ref[core, ENTRY])
    def _(t):
        pair = tab_ref[core, ENTRY + 1 + t]
        a, b = pair >> 3, pair & 7
        mine, other = jnp.where(core == 0, a, b), jnp.where(core == 0, b, a)
        add_terms(u_ref, sib_ref, acc_ref, kacc_ref, mine, other)


def run_tasks(stage, size, task_ref, u_ref, q_ref, acc_ref, kacc_ref):
    def per_block(own, carry):
        row = stage * BPD + own

        def step(t, inner):
            place = task_ref[TASK + row * 64 + t]
            add_terms(
                u_ref, q_ref, acc_ref, kacc_ref, own, (place >> 8) * size + (place & 255)
            )
            return inner

        lax.fori_loop(0, task_ref[TASKS + row], step, 0)
        return carry

    lax.fori_loop(0, BPD, per_block, 0)


def fetch(size, sources, q_ref, sems):
    copies = [
        pltpu.make_async_copy(
            source, q_ref.at[n * size * BLOCK : (n + 1) * size * BLOCK, :], sems.at[n]
        )
        for n, source in enumerate(sources)
    ]
    for copy in copies:
        copy.start()
    for copy in copies:
        copy.wait()


def near_kernel(size, task_ref, u_ref, acc_in, kacc_in, g0, g1, g2, g3, acc_ref, kacc_ref, q_ref, sems):
    acc_ref[...] = acc_in[...]
    kacc_ref[...] = kacc_in[...]
    fetch(size, (g0, g1, g2, g3), q_ref, sems)
    run_tasks(0, size, task_ref, u_ref, q_ref, acc_ref, kacc_ref)


def last_kernel(
    size, task_ref, u_ref, acc_in, kacc_in, g0, g1, g2, g3, out_ref, log_ref, acc_ref, kacc_ref, done_ref, q_ref, sems, out_sems
):
    fetch(size, (g0, g1, g2, g3), q_ref, sems)
    rows = lax.broadcasted_iota(jnp.int32, (BLOCK, BLOCK), 0)
    diagonal = rows == lax.broadcasted_iota(jnp.int32, (BLOCK, BLOCK), 1)

    def out_copy(own):
        return pltpu.make_async_copy(
            done_ref.at[rows_of(own), :], out_ref.at[rows_of(own), :], out_sems.at[own]
        )

    @functools.partial(loop, BPD)
    def _(own):
        row = BPD + own
        acc_ref[...] = acc_in[rows_of(own), :]
        kacc_ref[...] = kacc_in[rows_of(own), :]

        @functools.partial(loop, task_ref[TASKS + row])
        def _(t):
            place = task_ref[TASK + row * 64 + t]
            other = (place >> 8) * size + (place & 255)
            q = q_ref[rows_of(other), :]
            kernel = kernel_values(u_ref[rows_of(own), :], q)
            kacc_ref[...] += kernel
            acc_ref[...] += jnp.dot(kernel.astype(jnp.bfloat16), q, preferred_element_type=jnp.float32)

        density = jnp.sum(kacc_ref[...], axis=1, keepdims=True)
        done_ref[rows_of(own), :] = (
            u_ref[rows_of(own), :].astype(jnp.float32) - acc_ref[...] * (1.0 / density)
        ).astype(jnp.bfloat16)
        out_copy(own).start()
        across = jnp.sum(jnp.where(diagonal, density, 0.0), axis=0, keepdims=True)
        log_ref[pl.ds(own, 1), :] = jnp.log(across)

    for own in range(BPD):
        out_copy(own).wait()


SMEM = pl.BlockSpec(memory_space=pltpu.SMEM)
VMEM = pl.BlockSpec(memory_space=pltpu.VMEM)
ANY = pl.BlockSpec(memory_space=pl.ANY)


def params(mib):
    return pltpu.CompilerParams(vmem_limit_bytes=mib * 2**20)


def cost(pairs, width):
    return pl.CostEstimate(
        flops=pairs * 4 * BLOCK * BLOCK * width, bytes_accessed=8 * 2**20, transcendentals=pairs * BLOCK * BLOCK
    )


def exchange_and_score(first, second, pos, plan, tables, surplus, unit, sib):
    rows, width = unit.shape
    sends = lambda size: tuple(jax.ShapeDtypeStruct((size * BLOCK, width), jnp.bfloat16) for _ in range(2))
    sums = (
        jax.ShapeDtypeStruct((rows, width), jnp.float32),
        jax.ShapeDtypeStruct((rows, BLOCK), jnp.float32),
    )
    up, down = pl.pallas_call(
        functools.partial(first_pack_kernel, first),
        in_specs=[SMEM, SMEM, ANY, ANY],
        out_specs=(VMEM, VMEM),
        out_shape=sends(first),
        scratch_shapes=[pltpu.SemaphoreType.DMA((2 * first,))],
        compiler_params=params(8 + first),
        name="first_pack",
    )(pos, plan, unit, sib)
    got_up, got_down = along_chips(up, 1), along_chips(down, -1)

    places = pl.pallas_call(
        places_kernel,
        in_specs=[SMEM, SMEM, SMEM],
        out_specs=SMEM,
        out_shape=jax.ShapeDtypeStruct((PLACES,), jnp.int32),
        cost_estimate=cost(16, width),
        name="places",
    )(pos, tables, plan)
    acc, kacc = pl.pallas_call(
        own_kernel,
        in_specs=[SMEM, SMEM, SMEM, VMEM, VMEM],
        out_specs=(VMEM, VMEM),
        out_shape=sums,
        scratch_shapes=[pltpu.SMEM((BPD * BPD,), jnp.float32)],
        compiler_params=params(20),
        cost_estimate=cost(64, width),
        name="own_pairs",
    )(pos, tables, surplus, unit, sib)

    got_up, got_down, acc, places = lax.optimization_barrier((got_up, got_down, acc, places))
    up, down = pl.pallas_call(
        functools.partial(second_pack_kernel, first, second),
        in_specs=[SMEM, SMEM] + [ANY] * 4,
        out_specs=(VMEM, VMEM),
        out_shape=sends(second),
        scratch_shapes=[pltpu.SemaphoreType.DMA((2 * second,))],
        compiler_params=params(8 + second),
        name="second_pack",
    )(pos, plan, unit, sib, got_up, got_down)
    far_up, far_down = along_chips(up, 1), along_chips(down, -1)
    got_up, got_down, _, _ = lax.optimization_barrier((got_up, got_down, up, down))
    sib_up, sib_down = to_sibling(got_up), to_sibling(got_down)

    acc, kacc = pl.pallas_call(
        functools.partial(near_kernel, first),
        in_specs=[SMEM, VMEM, VMEM, VMEM] + [ANY] * 4,
        out_specs=(VMEM, VMEM),
        out_shape=sums,
        scratch_shapes=[
            pltpu.VMEM((4 * first * BLOCK, width), jnp.bfloat16),
            pltpu.SemaphoreType.DMA((4,)),
        ],
        compiler_params=params(16 + first),
        cost_estimate=cost(12, width),
        name="near_pairs",
    )(places, unit, acc, kacc, got_up, sib_up, got_down, sib_down)

    far_up, far_down, acc = lax.optimization_barrier((far_up, far_down, acc))
    far_sib_up, far_sib_down = to_sibling(far_up), to_sibling(far_down)
    centered, log_density = pl.pallas_call(
        functools.partial(last_kernel, second),
        in_specs=[SMEM, VMEM, VMEM, VMEM] + [ANY] * 4,
        out_specs=(ANY, VMEM),
        out_shape=(
            jax.ShapeDtypeStruct((rows, width), jnp.bfloat16),
            jax.ShapeDtypeStruct((BPD, BLOCK), jnp.float32),
        ),
        scratch_shapes=[
            pltpu.VMEM((BLOCK, width), jnp.float32),
            pltpu.VMEM((BLOCK, BLOCK), jnp.float32),
            pltpu.VMEM((rows, width), jnp.bfloat16),
            pltpu.VMEM((4 * second * BLOCK, width), jnp.bfloat16),
            pltpu.SemaphoreType.DMA((4,)),
            pltpu.SemaphoreType.DMA((BPD,)),
        ],
        compiler_params=params(16 + second),
        cost_estimate=cost(8, width),
        name="far_pairs",
    )(places, unit, acc, kacc, far_up, far_sib_up, far_down, far_sib_down)
    return centered, log_density


def shards(embeddings, home_pairs, home_count, surplus_pairs):
    rows, width = embeddings.shape
    pairs, count = home_pairs[0, 0], home_count[0, 0]
    shifts = pairs.shape[0]
    pos = lax.axis_index("owner").astype(jnp.int32).reshape(1)

    step = 128
    unit = pl.pallas_call(
        normalize_kernel,
        grid=(rows // step,),
        in_specs=[pl.BlockSpec((step, width), lambda i: (i, 0))],
        out_specs=pl.BlockSpec((step, width), lambda i: (i, 0)),
        out_shape=jax.ShapeDtypeStruct(embeddings.shape, jnp.bfloat16),
        cost_estimate=pl.CostEstimate(flops=2**22, bytes_accessed=2**22, transcendentals=1024),
        name="normalize",
    )(embeddings)

    packed = jnp.concatenate([count[:, None], pairs[:, :MOST, 0] * 8 + pairs[:, :MOST, 1]], axis=1)
    tables = jnp.pad(packed.reshape(1, -1), ((0, 0), (0, 128 - shifts * ENTRY)))
    for bit in (1, 2, 4):
        route = [(o, o ^ bit) for o in range(OWNERS)]
        came = lax.ppermute(tables, "owner", route)
        if bit == 1:
            came, unit = lax.optimization_barrier((came, unit))
            sib = to_sibling(unit)
        tables = jnp.concatenate([tables, came], axis=0)

    plan, chosen = pl.pallas_call(
        plan_kernel,
        in_specs=[SMEM, SMEM],
        out_specs=(SMEM, SMEM),
        out_shape=(
            jax.ShapeDtypeStruct((PLAN,), jnp.int32),
            jax.ShapeDtypeStruct((1,), jnp.int32),
        ),
        name="plan",
    )(pos, tables)

    centered, log_density = lax.switch(
        chosen[0],
        [functools.partial(exchange_and_score, *size) for size in SIZES],
        pos, plan, tables, surplus_pairs[0, 0], unit, sib,
    )
    return centered, log_density.reshape(rows)


def solution(mesh):
    return jax.shard_map(
        shards,
        mesh=mesh,
        in_specs=(
            P(("group", "owner"), None),
            P("group", "owner", None, None, None),
            P("group", "owner", None),
            P("group", "owner", None, None),
        ),
        out_specs=(P(("group", "owner"), None), P(("group", "owner"))),
        check_vma=False,
    )
```

profile of v0, /device:TPU:1, one launch (start us, length us, event | category | flops | bytes accessed | tf_op | source)
XLA Modules:
  0.0 77.7 jit_solution(491447716925824252)
XLA Ops:
  0.6 0.7 copy.16
  1.4 0.7 copy.27
  2.2 1.5 %collective-permute-start.24 = (s32[1,128]{1,0:T(1,128)S(1)}, s32[1,128]{1,0:T(1,128)S(1)}, u32[]{:S(2)}, u32[]{:S(2)}) collective-permute-start(s32[1,128]{1,0:T(1,128)S(1)} %pad.4), channel_id=1, source_target_pairs={{0,1},{1,0},{2,3},{3,2},{4,5},{5,4},{6,7},{7,6},{8,9},{9,8},{10,11... | collective-permute-start | bytes 1544 | tf_op jit(solution)/shard_map/ppermute | solution.py:531
  3.7 4.6 %normalize.1 = bf16[1024,1024]{1,0:T(8,128)(2,1)S(1)} custom-call(bf16[1024,1024]{1,0:T(8,128)(2,1)} %x_ref.1), custom_call_target="tpu_custom_call" | custom-call | flops 4194304 | bytes 4194304 | tf_op jit(solution)/shard_map/normalize/pallas_call | solution.py:517
  8.4 0.1 collective-permute-start.27
  8.5 1.5 %collective-permute-start.25 = (s32[2,128]{1,0:T(2,128)S(1)}, s32[2,128]{1,0:T(2,128)S(1)}, u32[]{:S(2)}, u32[]{:S(2)}) collective-permute-start(s32[2,128]{1,0:T(2,128)S(1)} %pad_add_fusion.3), channel_id=1, source_target_pairs={{0,2},{1,3},{2,0},{3,1},{4,6},{5,7},{6,4},{7,5},{8,10},{9,11},{10,... | collective-permute-start | bytes 3080 | tf_op jit(solution)/shard_map/ppermute | solution.py:531
  9.9 1.0 %collective-permute-done.25 = s32[2,128]{1,0:T(2,128)S(1)} collective-permute-done((s32[2,128]{1,0:T(2,128)S(1)}, s32[2,128]{1,0:T(2,128)S(1)}, u32[]{:S(2)}, u32[]{:S(2)}) %collective-permute-start.25) | collective-permute-done | bytes 1056 | tf_op jit(solution)/shard_map/ppermute | solution.py:531
  11.0 3.1 %collective-permute-start.26 = (s32[4,128]{1,0:T(4,128)S(1)}, s32[4,128]{1,0:T(4,128)S(1)}, u32[]{:S(2)}, u32[]{:S(2)}) collective-permute-start(s32[4,128]{1,0:T(4,128)S(1)} %pad_add_fusion.2), channel_id=1, source_target_pairs={{0,4},{1,5},{2,6},{3,7},{4,0},{5,1},{6,2},{7,3},{8,12},{9,13},{10,... | collective-permute-start | bytes 6152 | tf_op jit(solution)/shard_map/ppermute | solution.py:531
  14.1 1.0 %collective-permute-done.26 = s32[4,128]{1,0:T(4,128)S(1)} collective-permute-done((s32[4,128]{1,0:T(4,128)S(1)}, s32[4,128]{1,0:T(4,128)S(1)}, u32[]{:S(2)}, u32[]{:S(2)}) %collective-permute-start.26) | collective-permute-done | bytes 2080 | tf_op jit(solution)/shard_map/ppermute | solution.py:531
  15.0 4.1 %plan.1 = (s32[768]{0:T(1024)S(1)}, s32[1]{0:T(128)}) custom-call(s32[1]{0:T(128)} %bitcast.6.pos_ref, s32[8,128]{1,0:T(8,128)S(1)} %pad_add_fusion.1.tab_ref), custom_call_target="tpu_custom_call" | custom-call | tf_op jit(solution)/shard_map/plan/pallas_call | solution.py:537
  19.8 57.7 %conditional.1 = (bf16[1024,1024]{1,0:T(8,128)(2,1)}, f32[1024]{0:T(1024)}) conditional(s32[]{:T(128)} %bitcast.10, (s32[1]{0:T(128)}, s32[768]{0:T(1024)S(1)}, bf16[1024,1024]{1,0:T(8,128)(2,1)S(1)}, bf16[1024,1024]{1,0:T(8,128)(2,1)}, s32[1,1,16,3]{2,1,3,0:T(1,128)S(1)}, /*index=5*/s32[8,128]{1,0:T(8,128)S(1)}) %tuple.43, ...), branch_computations={%region_0.1_spmd, %region_1.2_spmd, %region_2.3_spmd} | conditional | flops 6710886400 | bytes 117460128 | solution.py:548
  19.8 1.3 %copy-done.3 = bf16[1024,1024]{1,0:T(8,128)(2,1)} copy-done((bf16[1024,1024]{1,0:T(8,128)(2,1)}, bf16[1024,1024]{1,0:T(8,128)(2,1)S(1)}, u32[]{:S(2)}) %copy-start.3) | copy-done | bytes 2097176 | tf_op jit(solution)/shard_map/cond
  21.1 2.0 %first_pack.3 = (bf16[384,1024]{1,0:T(8,128)(2,1)S(1)}, bf16[384,1024]{1,0:T(8,128)(2,1)S(1)}) custom-call(s32[1]{0:T(128)} %get-tuple-element.46.pos_ref, s32[768]{0:T(1024)S(1)} %get-tuple-element.47.plan_ref, bf16[1024,1024]{1,0:T(8,128)(2,1)} %copy-done.3, bf16[1024,1024]{1,0:T(8,128)(2,1)} %get-tuple-element.49.sib_ref), custom_call_target="tpu_custom_call" | custom-call | tf_op jit(solution)/shard_map/cond/branch_0_fun/first_pack/pallas_call | solution.py:427
  23.1 1.5 %collective-permute-start = (bf16[384,1024]{1,0:T(8,128)(2,1)S(1)}, bf16[384,1024]{1,0:T(8,128)(2,1)S(1)}, u32[]{:S(2)}, u32[]{:S(2)}) collective-permute-start(bf16[384,1024]{1,0:T(8,128)(2,1)S(1)} %get-tuple-element.50), channel_id=1, source_target_pairs={{0,2},{1,3},{2,4},{3,5},{4,6},{5,7},{6,0},{7,1},{8,10},{9,11},{10,... | collective-permute-start | bytes 2359304 | tf_op jit(solution)/shard_map/cond/branch_0_fun/ppermute | solution.py:39
  24.6 1.5 %collective-permute-start.1 = (bf16[384,1024]{1,0:T(8,128)(2,1)S(1)}, bf16[384,1024]{1,0:T(8,128)(2,1)S(1)}, u32[]{:S(2)}, u32[]{:S(2)}) collective-permute-start(bf16[384,1024]{1,0:T(8,128)(2,1)S(1)} %get-tuple-element.51), channel_id=1, source_target_pairs={{0,6},{1,7},{2,0},{3,1},{4,2},{5,3},{6,4},{7,5},{8,14},{9,15},{10,... | collective-permute-start | bytes 2359304 | tf_op jit(solution)/shard_map/cond/branch_0_fun/ppermute | solution.py:39
  26.1 0.1 copy.12.surplus_ref
  26.2 1.6 %places.3.task_ref = s32[1152]{0:T(1024)} custom-call(s32[1]{0:T(128)} %get-tuple-element.46.pos_ref, s32[8,128]{1,0:T(8,128)S(1)} %get-tuple-element.52.tab_ref, s32[768]{0:T(1024)S(1)} %get-tuple-element.47.plan_ref), custom_call_target="tpu_custom_call" | custom-call | flops 1073741824 | bytes 8388608 | tf_op jit(solution)/shard_map/cond/branch_0_fun/places/pallas_call | solution.py:438
  27.8 8.4 %own_pairs.3 = (f32[1024,1024]{1,0:T(8,128)S(1)}, f32[1024,128]{1,0:T(8,128)S(1)}) custom-call(s32[1]{0:T(128)} %get-tuple-element.46.pos_ref, s32[8,128]{1,0:T(8,128)S(1)} %get-tuple-element.52.tab_ref, s32[16,3]{1,0:T(8,128)S(1)} %copy.12.surplus_ref, bf16[1024,1024]{1,0:T(8,128)(2,1)} %copy-done.3, bf16[1024,1024]{1,0:T(8,128)(2,1)} %get-tuple-element.49.sib_ref), custom_call_target="tpu_custom_call" | custom-call | flops 4294967296 | bytes 8388608 | tf_op jit(solution)/shard_map/cond/branch_0_fun/own_pairs/pallas_call | solution.py:446
  36.3 4.7 %collective-permute-done.got_up.g0 = bf16[384,1024]{1,0:T(8,128)(2,1)S(1)} collective-permute-done((bf16[384,1024]{1,0:T(8,128)(2,1)S(1)}, bf16[384,1024]{1,0:T(8,128)(2,1)S(1)}, u32[]{:S(2)}, u32[]{:S(2)}) %collective-permute-start) | collective-permute-done | bytes 786464 | tf_op jit(solution)/shard_map/cond/branch_0_fun/ppermute | solution.py:39
  41.0 1.9 %second_pack.3 = (bf16[384,1024]{1,0:T(8,128)(2,1)S(1)}, bf16[384,1024]{1,0:T(8,128)(2,1)S(1)}) custom-call(s32[1]{0:T(128)} %get-tuple-element.46.pos_ref, s32[768]{0:T(1024)S(1)} %get-tuple-element.47.plan_ref, bf16[1024,1024]{1,0:T(8,128)(2,1)S(1)} %copy-done.4, bf16[1024,1024]{1,0:T(8,128)(2,1)} %get-tuple-element.49.sib_ref, ...), custom_call_target="tpu_custom_call" | custom-call | tf_op jit(solution)/shard_map/cond/branch_0_fun/second_pack/pallas_call | solution.py:458
  43.0 2.6 %collective-permute-start.4 = (bf16[384,1024]{1,0:T(8,128)(2,1)S(1)}, bf16[384,1024]{1,0:T(8,128)(2,1)S(1)}, u32[]{:S(2)}, u32[]{:S(2)}) collective-permute-start(bf16[384,1024]{1,0:T(8,128)(2,1)S(1)} %collective-permute-done.got_up.g0), channel_id=1, source_target_pairs={{0,1},{1,0},{2,3},{3,2},{4,5},{5,4},{6,7},{7,6},{8,9},{9,8},{10,11... | collective-permute-start | bytes 2359304 | tf_op jit(solution)/shard_map/cond/branch_0_fun/ppermute | solution.py:43
  45.5 0.1 collective-permute-start.5
  45.6 1.2 %collective-permute-start.2 = (bf16[384,1024]{1,0:T(8,128)(2,1)S(1)}, bf16[384,1024]{1,0:T(8,128)(2,1)S(1)}, u32[]{:S(2)}, u32[]{:S(2)}) collective-permute-start(bf16[384,1024]{1,0:T(8,128)(2,1)S(1)} %get-tuple-element.58), channel_id=1, source_target_pairs={{0,2},{1,3},{2,4},{3,5},{4,6},{5,7},{6,0},{7,1},{8,10},{9,11},{10,... | collective-permute-start | bytes 2359304 | tf_op jit(solution)/shard_map/cond/branch_0_fun/ppermute | solution.py:39
  46.9 1.4 %collective-permute-start.3 = (bf16[384,1024]{1,0:T(8,128)(2,1)S(1)}, bf16[384,1024]{1,0:T(8,128)(2,1)S(1)}, u32[]{:S(2)}, u32[]{:S(2)}) collective-permute-start(bf16[384,1024]{1,0:T(8,128)(2,1)S(1)} %get-tuple-element.59), channel_id=1, source_target_pairs={{0,6},{1,7},{2,0},{3,1},{4,2},{5,3},{6,4},{7,5},{8,14},{9,15},{10,... | collective-permute-start | bytes 2359304 | tf_op jit(solution)/shard_map/cond/branch_0_fun/ppermute | solution.py:39
  48.3 0.3 collective-permute-done.5.g3
  48.6 3.3 %near_pairs.3 = (f32[1024,1024]{1,0:T(8,128)S(1)}, f32[1024,128]{1,0:T(8,128)S(1)}) custom-call(s32[1152]{0:T(1024)S(1)} %copy-done.2, bf16[1024,1024]{1,0:T(8,128)(2,1)S(1)} %copy-done.4, f32[1024,1024]{1,0:T(8,128)S(1)} %get-tuple-element.60.acc_in, f32[1024,128]{1,0:T(8,128)S(1)} %get-tuple-element.61.kacc_in, ...), custom_call_target="tpu_custom_call" | custom-call | flops 805306368 | bytes 8388608 | tf_op jit(solution)/shard_map/cond/branch_0_fun/near_pairs/pallas_call | solution.py:471
  51.9 13.6 %collective-permute-done.2.g0 = bf16[384,1024]{1,0:T(8,128)(2,1)S(1)} collective-permute-done((bf16[384,1024]{1,0:T(8,128)(2,1)S(1)}, bf16[384,1024]{1,0:T(8,128)(2,1)S(1)}, u32[]{:S(2)}, u32[]{:S(2)}) %collective-permute-start.2) | collective-permute-done | bytes 786464 | tf_op jit(solution)/shard_map/cond/branch_0_fun/ppermute | solution.py:39
  65.5 0.5 collective-permute-done.3.g2
  66.0 1.3 %collective-permute-start.6 = (bf16[384,1024]{1,0:T(8,128)(2,1)S(1)}, bf16[384,1024]{1,0:T(8,128)(2,1)S(1)}, u32[]{:S(2)}, u32[]{:S(2)}) collective-permute-start(bf16[384,1024]{1,0:T(8,128)(2,1)S(1)} %collective-permute-done.2.g0), channel_id=1, source_target_pairs={{0,1},{1,0},{2,3},{3,2},{4,5},{5,4},{6,7},{7,6},{8,9},{9,8},{10,11... | collective-permute-start | bytes 2359304 | tf_op jit(solution)/shard_map/cond/branch_0_fun/ppermute | solution.py:43
  67.3 1.9 %collective-permute-done.6.g1 = bf16[384,1024]{1,0:T(8,128)(2,1)S(1)} collective-permute-done((bf16[384,1024]{1,0:T(8,128)(2,1)S(1)}, bf16[384,1024]{1,0:T(8,128)(2,1)S(1)}, u32[]{:S(2)}, u32[]{:S(2)}) %collective-permute-start.6) | collective-permute-done | bytes 786464 | tf_op jit(solution)/shard_map/cond/branch_0_fun/ppermute | solution.py:43
  69.2 1.1 %collective-permute-done.7.g3 = bf16[384,1024]{1,0:T(8,128)(2,1)S(1)} collective-permute-done((bf16[384,1024]{1,0:T(8,128)(2,1)S(1)}, bf16[384,1024]{1,0:T(8,128)(2,1)S(1)}, u32[]{:S(2)}, u32[]{:S(2)}) %collective-permute-start.7) | collective-permute-done | bytes 786464 | tf_op jit(solution)/shard_map/cond/branch_0_fun/ppermute | solution.py:43
  70.3 6.9 %far_pairs.3 = (bf16[1024,1024]{1,0:T(8,128)(2,1)}, f32[8,128]{1,0:T(8,128)}) custom-call(s32[1152]{0:T(1024)S(1)} %copy-done.2, bf16[1024,1024]{1,0:T(8,128)(2,1)S(1)} %copy-done.4, f32[1024,1024]{1,0:T(8,128)S(1)} %get-tuple-element.65.acc_in, f32[1024,128]{1,0:T(8,128)S(1)} %get-tuple-element.66.kacc_in, bf16[384,1024]{1,0:T(8,128)(2,1)S(1)} %collective-permute-done.2.g0, ...), custom_call_target="tpu_custom_call" | custom-call | flops 536870912 | bytes 8388608 | tf_op jit(solution)/shard_map/cond/branch_0_fun/far_pairs/pallas_call | solution.py:487
  (20 shorter events, 0.2 us)
Async XLA Ops:
  2.2 17.5 %copy-start.9 = (s32[1,1,16,3]{2,1,3,0:T(1,128)S(1)}, s32[1,1,16,3]{2,1,3,0:T(1,128)}, u32[]{:S(2)}) copy-start(s32[1,1,16,3]{2,1,3,0:T(1,128)} %param.10) | copy-start | bytes 580
  2.2 6.1 %collective-permute-start.24 = (s32[1,128]{1,0:T(1,128)S(1)}, s32[1,128]{1,0:T(1,128)S(1)}, u32[]{:S(2)}, u32[]{:S(2)}) collective-permute-start(s32[1,128]{1,0:T(1,128)S(1)} %pad.4), channel_id=1, source_target_pairs={{0,1},{1,0},{2,3},{3,2},{4,5},{5,4},{6,7},{7,6},{8,9},{9,8},{10,11... | collective-permute-start | bytes 1544 | tf_op jit(solution)/shard_map/ppermute | solution.py:531
  8.4 11.4 %collective-permute-start.27 = (bf16[1024,1024]{1,0:T(8,128)(2,1)S(1)}, bf16[1024,1024]{1,0:T(8,128)(2,1)}, u32[]{:S(2)}, u32[]{:S(2)}) collective-permute-start(bf16[1024,1024]{1,0:T(8,128)(2,1)S(1)} %normalize.1), channel_id=1, source_target_pairs={{0,1},{1,0},{2,3},{3,2},{4,5},{5,4},{6,7},{7,6},{8,9},{9,8},{10,11... | collective-permute-start | bytes 6291464 | tf_op jit(solution)/shard_map/ppermute | solution.py:43
  8.5 2.5 %collective-permute-start.25 = (s32[2,128]{1,0:T(2,128)S(1)}, s32[2,128]{1,0:T(2,128)S(1)}, u32[]{:S(2)}, u32[]{:S(2)}) collective-permute-start(s32[2,128]{1,0:T(2,128)S(1)} %pad_add_fusion.3), channel_id=1, source_target_pairs={{0,2},{1,3},{2,0},{3,1},{4,6},{5,7},{6,4},{7,5},{8,10},{9,11},{10,... | collective-permute-start | bytes 3080 | tf_op jit(solution)/shard_map/ppermute | solution.py:531
  11.0 4.0 %collective-permute-start.26 = (s32[4,128]{1,0:T(4,128)S(1)}, s32[4,128]{1,0:T(4,128)S(1)}, u32[]{:S(2)}, u32[]{:S(2)}) collective-permute-start(s32[4,128]{1,0:T(4,128)S(1)} %pad_add_fusion.2), channel_id=1, source_target_pairs={{0,4},{1,5},{2,6},{3,7},{4,0},{5,1},{6,2},{7,3},{8,12},{9,13},{10,... | collective-permute-start | bytes 6152 | tf_op jit(solution)/shard_map/ppermute | solution.py:531
  19.8 1.3 %copy-start.3 = (bf16[1024,1024]{1,0:T(8,128)(2,1)}, bf16[1024,1024]{1,0:T(8,128)(2,1)S(1)}, u32[]{:S(2)}) copy-start(bf16[1024,1024]{1,0:T(8,128)(2,1)S(1)} %get-tuple-element.48.unit_ref.u_ref) | copy-start | bytes 6291460 | tf_op jit(solution)/shard_map/cond
  23.1 17.9 %collective-permute-start = (bf16[384,1024]{1,0:T(8,128)(2,1)S(1)}, bf16[384,1024]{1,0:T(8,128)(2,1)S(1)}, u32[]{:S(2)}, u32[]{:S(2)}) collective-permute-start(bf16[384,1024]{1,0:T(8,128)(2,1)S(1)} %get-tuple-element.50), channel_id=1, source_target_pairs={{0,2},{1,3},{2,4},{3,5},{4,6},{5,7},{6,0},{7,1},{8,10},{9,11},{10,... | collective-permute-start | bytes 2359304 | tf_op jit(solution)/shard_map/cond/branch_0_fun/ppermute | solution.py:39
  24.6 16.4 %collective-permute-start.1 = (bf16[384,1024]{1,0:T(8,128)(2,1)S(1)}, bf16[384,1024]{1,0:T(8,128)(2,1)S(1)}, u32[]{:S(2)}, u32[]{:S(2)}) collective-permute-start(bf16[384,1024]{1,0:T(8,128)(2,1)S(1)} %get-tuple-element.51), channel_id=1, source_target_pairs={{0,6},{1,7},{2,0},{3,1},{4,2},{5,3},{6,4},{7,5},{8,14},{9,15},{10,... | collective-permute-start | bytes 2359304 | tf_op jit(solution)/shard_map/cond/branch_0_fun/ppermute | solution.py:39
  27.8 13.2 %copy-start.4 = (bf16[1024,1024]{1,0:T(8,128)(2,1)S(1)}, bf16[1024,1024]{1,0:T(8,128)(2,1)}, u32[]{:S(2)}) copy-start(bf16[1024,1024]{1,0:T(8,128)(2,1)} %copy-done.3) | copy-start | bytes 6291460 | tf_op jit(solution)/shard_map/cond
  41.0 7.6 %copy-start.2 = (s32[1152]{0:T(1024)S(1)}, s32[1152]{0:T(1024)}, u32[]{:S(2)}) copy-start(s32[1152]{0:T(1024)} %places.3.task_ref) | copy-start | bytes 13828 | tf_op jit(solution)/shard_map/cond
  43.0 5.3 %collective-permute-start.4 = (bf16[384,1024]{1,0:T(8,128)(2,1)S(1)}, bf16[384,1024]{1,0:T(8,128)(2,1)S(1)}, u32[]{:S(2)}, u32[]{:S(2)}) collective-permute-start(bf16[384,1024]{1,0:T(8,128)(2,1)S(1)} %collective-permute-done.got_up.g0), channel_id=1, source_target_pairs={{0,1},{1,0},{2,3},{3,2},{4,5},{5,4},{6,7},{7,6},{8,9},{9,8},{10,11... | collective-permute-start | bytes 2359304 | tf_op jit(solution)/shard_map/cond/branch_0_fun/ppermute | solution.py:43
  45.5 3.0 %collective-permute-start.5 = (bf16[384,1024]{1,0:T(8,128)(2,1)S(1)}, bf16[384,1024]{1,0:T(8,128)(2,1)S(1)}, u32[]{:S(2)}, u32[]{:S(2)}) collective-permute-start(bf16[384,1024]{1,0:T(8,128)(2,1)S(1)} %collective-permute-done.1.got_down.g2), channel_id=1, source_target_pairs={{0,1},{1,0},{2,3},{3,2},{4,5},{5,4},{6,7},{7,6},{8,9},{9,8},{10,11... | collective-permute-start | bytes 2359304 | tf_op jit(solution)/shard_map/cond/branch_0_fun/ppermute | solution.py:43
  45.6 19.9 %collective-permute-start.2 = (bf16[384,1024]{1,0:T(8,128)(2,1)S(1)}, bf16[384,1024]{1,0:T(8,128)(2,1)S(1)}, u32[]{:S(2)}, u32[]{:S(2)}) collective-permute-start(bf16[384,1024]{1,0:T(8,128)(2,1)S(1)} %get-tuple-element.58), channel_id=1, source_target_pairs={{0,2},{1,3},{2,4},{3,5},{4,6},{5,7},{6,0},{7,1},{8,10},{9,11},{10,... | collective-permute-start | bytes 2359304 | tf_op jit(solution)/shard_map/cond/branch_0_fun/ppermute | solution.py:39
  46.9 19.1 %collective-permute-start.3 = (bf16[384,1024]{1,0:T(8,128)(2,1)S(1)}, bf16[384,1024]{1,0:T(8,128)(2,1)S(1)}, u32[]{:S(2)}, u32[]{:S(2)}) collective-permute-start(bf16[384,1024]{1,0:T(8,128)(2,1)S(1)} %get-tuple-element.59), channel_id=1, source_target_pairs={{0,6},{1,7},{2,0},{3,1},{4,2},{5,3},{6,4},{7,5},{8,14},{9,15},{10,... | collective-permute-start | bytes 2359304 | tf_op jit(solution)/shard_map/cond/branch_0_fun/ppermute | solution.py:39
  66.0 3.2 %collective-permute-start.6 = (bf16[384,1024]{1,0:T(8,128)(2,1)S(1)}, bf16[384,1024]{1,0:T(8,128)(2,1)S(1)}, u32[]{:S(2)}, u32[]{:S(2)}) collective-permute-start(bf16[384,1024]{1,0:T(8,128)(2,1)S(1)} %collective-permute-done.2.g0), channel_id=1, source_target_pairs={{0,1},{1,0},{2,3},{3,2},{4,5},{5,4},{6,7},{7,6},{8,9},{9,8},{10,11... | collective-permute-start | bytes 2359304 | tf_op jit(solution)/shard_map/cond/branch_0_fun/ppermute | solution.py:43
  67.3 3.0 %collective-permute-start.7 = (bf16[384,1024]{1,0:T(8,128)(2,1)S(1)}, bf16[384,1024]{1,0:T(8,128)(2,1)S(1)}, u32[]{:S(2)}, u32[]{:S(2)}) collective-permute-start(bf16[384,1024]{1,0:T(8,128)(2,1)S(1)} %collective-permute-done.3.g2), channel_id=1, source_target_pairs={{0,1},{1,0},{2,3},{3,2},{4,5},{5,4},{6,7},{7,6},{8,9},{9,8},{10,11... | collective-permute-start | bytes 2359304 | tf_op jit(solution)/shard_map/cond/branch_0_fun/ppermute | solution.py:43
where the time goes:
time: 77.4 us; the launch traced here: 77.7 us
  Pallas kernels  33 us (43%)
  waiting for transfers between devices  24.1 us (31%)
  starting transfers between devices  15.6 us (20%)
  local copies, waits for them, and re-layouts  2.94 us (4%)
  between operations  1.51 us (2%)
    ppermute x4, waiting for transfers between devices, along_chips(): return lax.ppermute(x, 'owner', route)  18.8 us
    pallas_call x1, Pallas kernels, exchange_and_score(): pl.pallas_call(own_kernel, in_specs=[SMEM, SMEM, SMEM, VMEM, VMEM], out_s...  8.44 us
    pallas_call x1, Pallas kernels, exchange_and_score(): pl.pallas_call(functools.partial(last_kernel, second), in_specs=[SMEM, VM...  6.94 us
    ppermute x3, starting transfers between devices, shards(): came = lax.ppermute(tables, 'owner', route)  6.03 us
    ppermute x4, starting transfers between devices, along_chips(): return lax.ppermute(x, 'owner', route)  5.6 us
    pallas_call x1, Pallas kernels, shards(): pl.pallas_call(normalize_kernel, grid=(rows // step,), in_specs=[pl.Block...  4.61 us
    pallas_call x1, Pallas kernels, shards(): pl.pallas_call(plan_kernel, in_specs=[SMEM, SMEM], out_specs=(SMEM, SMEM)...  4.08 us
    ppermute x5, starting transfers between devices, to_sibling(): return lax.ppermute(x, 'owner', [(o, o ^ 1) for o in range(OWNERS)])  4.01 us
  transfers between devices with their start and end apart: 12, of which 8 were waited for; matrix products, arithmetic and copies ran while one was open for 0% of the time, Pallas kernels for 28%

commit v1 on v0

--- a/solution.py
+++ b/solution.py
@@ -16,13 +16,13 @@
 sharpness = 4.0
 epsilon = 1e-06
 SIZES = ((3, 3), (4, 4), (8, 8))
-MOST = 20
-ENTRY = MOST + 1
+COUNTS = 5
 
 STRIDE = 32
 F_COUNT, D_COUNT, LOAD, FIRST, NEED, TOUCHED, FAR, F_LIST, D_LIST = 0, 8, 16, 24, 32, 96, 161, 256, 512
 PLAN = 768
-TASKS, TASK, PLACE = 0, 16, 1040
+TASKS, TASK, PLACE = 0, 32, 1056
+ROW = 32
 PLACES = 1152
 
 
@@ -67,7 +67,13 @@
     )
 
 
-def plan_kernel(pos_ref, tab_ref, plan_ref, class_ref):
+def plan_kernel(pos_ref, t0, t1, t2, t3, plan_ref, tab_ref, class_ref, sems):
+    copies = [
+        pltpu.make_async_copy(t, tab_ref.at[i * 16 : (i + 1) * 16, :], sems.at[i])
+        for i, t in enumerate((t0, t1, t2, t3))
+    ]
+    for copy in copies:
+        copy.start()
     me = pos_ref[0]
     for i in range(8):
         plan_ref[LOAD + i] = 0
@@ -75,15 +81,17 @@
         plan_ref[D_COUNT + i] = 0
     for i in range(BLOCKS):
         plan_ref[NEED + i] = 0
+    for copy in copies:
+        copy.wait()
 
     def of_owner(o, touched):
-        row = o ^ me
+        row = (o ^ me) * 8
         for s in range(1, 5):
             q = (o + s) & 7
             to_q, to_o = lax.shift_left(1, q >> 1), lax.shift_left(1, o >> 1)
 
             def of_pair(t, touched):
-                pair = tab_ref[row, s * ENTRY + 1 + t]
+                pair = tab_ref[row + s, t]
                 for block, chip in ((o * BPD + (pair >> 3), to_q), (q * BPD + (pair & 7), to_o)):
                     before = plan_ref[NEED + block]
                     plan_ref[NEED + block] = before | chip
@@ -91,7 +99,7 @@
                     touched = touched + (before == 0).astype(jnp.int32)
                 return touched
 
-            touched = lax.fori_loop(0, tab_ref[row, s * ENTRY], of_pair, touched)
+            touched = lax.fori_loop(0, tab_ref[row + COUNTS, s], of_pair, touched)
         return touched
 
     touched = lax.fori_loop(0, OWNERS, of_owner, 0)
@@ -161,12 +169,12 @@
     me = pos_ref[0]
     y, core = me >> 1, me & 1
     first_size = plan_ref[FIRST]
-    for i in range(16):
+    for i in range(32):
         out_ref[TASKS + i] = 0
 
     def put(block, stage, way, position):
         other = (position & 1) ^ core
-        out_ref[PLACE + block] = stage * 65536 + (way * 2 + other) * 256 + (position >> 1)
+        out_ref[PLACE + block] = (2 * stage + other) * 65536 + way * 256 + (position >> 1)
 
     for way in (0, 1):
         near = 2 * ((y + (3 if way == 0 else 1)) & 3) + way
@@ -190,7 +198,7 @@
         place = out_ref[PLACE + block]
         row = (place >> 16) * BPD + own
         count = out_ref[TASKS + row]
-        out_ref[TASK + row * 64 + count] = place & 65535
+        out_ref[TASK + row * ROW + count] = place & 65535
         out_ref[TASKS + row] = count + 1
 
     for s in range(1, 5):
@@ -198,18 +206,18 @@
 
         @pl.when((above >> 1) != y)
         def _():
-            @functools.partial(loop, tab_ref[0, s * ENTRY])
+            @functools.partial(loop, tab_ref[COUNTS, s])
             def _(t):
-                pair = tab_ref[0, s * ENTRY + 1 + t]
+                pair = tab_ref[s, t]
                 add_task(pair >> 3, above * BPD + (pair & 7))
 
         @pl.when((below >> 1) != y)
         def _():
-            row = below ^ me
-
-            @functools.partial(loop, tab_ref[row, s * ENTRY])
+            row = (below ^ me) * 8
+
+            @functools.partial(loop, tab_ref[row + COUNTS, s])
             def _(t):
-                pair = tab_ref[row, s * ENTRY + 1 + t]
+                pair = tab_ref[row + s, t]
                 add_task(pair & 7, below * BPD + (pair >> 3))
 
 
@@ -288,9 +296,9 @@
         live_ref[a * BPD + b] = 1.0
         live_ref[b * BPD + a] = 1.0
 
-    @functools.partial(loop, tab_ref[0, 0])
+    @functools.partial(loop, tab_ref[COUNTS, 0])
     def _(t):
-        pair = tab_ref[0, 1 + t]
+        pair = tab_ref[0, t]
         mark(pair >> 3, pair & 7)
 
     @functools.partial(loop, surplus_ref.shape[0])
@@ -318,81 +326,68 @@
             jnp.concatenate(rows, axis=0), u_ref[...], preferred_element_type=jnp.float32
         )
 
-    @functools.partial(loop, tab_ref[core, ENTRY])
+    @functools.partial(loop, tab_ref[core * 8 + COUNTS, 1])
     def _(t):
-        pair = tab_ref[core, ENTRY + 1 + t]
+        pair = tab_ref[core * 8 + 1, t]
         a, b = pair >> 3, pair & 7
         mine, other = jnp.where(core == 0, a, b), jnp.where(core == 0, b, a)
         add_terms(u_ref, sib_ref, acc_ref, kacc_ref, mine, other)
 
 
-def run_tasks(stage, size, task_ref, u_ref, q_ref, acc_ref, kacc_ref):
-    def per_block(own, carry):
-        row = stage * BPD + own
-
-        def step(t, inner):
-            place = task_ref[TASK + row * 64 + t]
-            add_terms(
-                u_ref, q_ref, acc_ref, kacc_ref, own, (place >> 8) * size + (place & 255)
-            )
-            return inner
-
-        lax.fori_loop(0, task_ref[TASKS + row], step, 0)
-        return carry
-
-    lax.fori_loop(0, BPD, per_block, 0)
-
-
-def fetch(size, sources, q_ref, sems):
-    copies = [
-        pltpu.make_async_copy(
-            source, q_ref.at[n * size * BLOCK : (n + 1) * size * BLOCK, :], sems.at[n]
-        )
-        for n, source in enumerate(sources)
-    ]
-    for copy in copies:
-        copy.start()
-    for copy in copies:
-        copy.wait()
-
-
-def near_kernel(size, task_ref, u_ref, acc_in, kacc_in, g0, g1, g2, g3, acc_ref, kacc_ref, q_ref, sems):
+def each_task(task_ref, part, own, got, body):
+    row = part * BPD + own
+
+    @functools.partial(loop, task_ref[TASKS + row])
+    def _(t):
+        place = task_ref[TASK + row * ROW + t]
+        for way, ref in enumerate(got):
+
+            @pl.when((place >> 8) == way)
+            def _():
+                body(ref[rows_of(place & 255), :])
+
+
+def part_kernel(part, task_ref, u_ref, acc_in, kacc_in, up_ref, down_ref, acc_ref, kacc_ref):
     acc_ref[...] = acc_in[...]
     kacc_ref[...] = kacc_in[...]
-    fetch(size, (g0, g1, g2, g3), q_ref, sems)
-    run_tasks(0, size, task_ref, u_ref, q_ref, acc_ref, kacc_ref)
+
+    @functools.partial(loop, BPD)
+    def _(own):
+        here = rows_of(own)
+
+        def add(q):
+            kernel = kernel_values(u_ref[here, :], q)
+            kacc_ref[here, :] += kernel
+            acc_ref[here, :] += jnp.dot(kernel.astype(jnp.bfloat16), q, preferred_element_type=jnp.float32)
+
+        each_task(task_ref, part, own, (up_ref, down_ref), add)
 
 
 def last_kernel(
-    size, task_ref, u_ref, acc_in, kacc_in, g0, g1, g2, g3, out_ref, log_ref, acc_ref, kacc_ref, done_ref, q_ref, sems, out_sems
+    part, task_ref, u_ref, acc_in, kacc_in, up_ref, down_ref, out_ref, log_ref, acc_ref, kacc_ref, done_ref, sems
 ):
-    fetch(size, (g0, g1, g2, g3), q_ref, sems)
     rows = lax.broadcasted_iota(jnp.int32, (BLOCK, BLOCK), 0)
     diagonal = rows == lax.broadcasted_iota(jnp.int32, (BLOCK, BLOCK), 1)
 
     def out_copy(own):
-        return pltpu.make_async_copy(
-            done_ref.at[rows_of(own), :], out_ref.at[rows_of(own), :], out_sems.at[own]
-        )
+        here = rows_of(own)
+        return pltpu.make_async_copy(done_ref.at[here, :], out_ref.at[here, :], sems.at[own])
 
     @functools.partial(loop, BPD)
     def _(own):
-        row = BPD + own
-        acc_ref[...] = acc_in[rows_of(own), :]
-        kacc_ref[...] = kacc_in[rows_of(own), :]
-
-        @functools.partial(loop, task_ref[TASKS + row])
-        def _(t):
-            place = task_ref[TASK + row * 64 + t]
-            other = (place >> 8) * size + (place & 255)
-            q = q_ref[rows_of(other), :]
-            kernel = kernel_values(u_ref[rows_of(own), :], q)
+        here = rows_of(own)
+        acc_ref[...] = acc_in[here, :]
+        kacc_ref[...] = kacc_in[here, :]
+
+        def add(q):
+            kernel = kernel_values(u_ref[here, :], q)
             kacc_ref[...] += kernel
             acc_ref[...] += jnp.dot(kernel.astype(jnp.bfloat16), q, preferred_element_type=jnp.float32)
 
+        each_task(task_ref, part, own, (up_ref, down_ref), add)
         density = jnp.sum(kacc_ref[...], axis=1, keepdims=True)
-        done_ref[rows_of(own), :] = (
-            u_ref[rows_of(own), :].astype(jnp.float32) - acc_ref[...] * (1.0 / density)
+        done_ref[here, :] = (
+            u_ref[here, :].astype(jnp.float32) - acc_ref[...] * (1.0 / density)
         ).astype(jnp.bfloat16)
         out_copy(own).start()
         across = jnp.sum(jnp.where(diagonal, density, 0.0), axis=0, keepdims=True)
@@ -426,11 +421,11 @@
     )
     up, down = pl.pallas_call(
         functools.partial(first_pack_kernel, first),
-        in_specs=[SMEM, SMEM, ANY, ANY],
+        in_specs=[SMEM, SMEM, VMEM, VMEM],
         out_specs=(VMEM, VMEM),
         out_shape=sends(first),
         scratch_shapes=[pltpu.SemaphoreType.DMA((2 * first,))],
-        compiler_params=params(8 + first),
+        compiler_params=params(16 + first),
         name="first_pack",
     )(pos, plan, unit, sib)
     got_up, got_down = along_chips(up, 1), along_chips(down, -1)
@@ -441,6 +436,7 @@
         out_specs=SMEM,
         out_shape=jax.ShapeDtypeStruct((PLACES,), jnp.int32),
         cost_estimate=cost(16, width),
+        compiler_params=params(4),
         name="places",
     )(pos, tables, plan)
     acc, kacc = pl.pallas_call(
@@ -457,36 +453,39 @@
     got_up, got_down, acc, places = lax.optimization_barrier((got_up, got_down, acc, places))
     up, down = pl.pallas_call(
         functools.partial(second_pack_kernel, first, second),
-        in_specs=[SMEM, SMEM] + [ANY] * 4,
+        in_specs=[SMEM, SMEM] + [VMEM] * 4,
         out_specs=(VMEM, VMEM),
         out_shape=sends(second),
         scratch_shapes=[pltpu.SemaphoreType.DMA((2 * second,))],
-        compiler_params=params(8 + second),
+        compiler_params=params(16 + second + first),
         name="second_pack",
     )(pos, plan, unit, sib, got_up, got_down)
     far_up, far_down = along_chips(up, 1), along_chips(down, -1)
+
+    def add_part(part, size, acc, kacc, from_below, from_above):
+        return pl.pallas_call(
+            functools.partial(part_kernel, part),
+            in_specs=[SMEM] + [VMEM] * 5,
+            out_specs=(VMEM, VMEM),
+            out_shape=sums,
+            compiler_params=params(16 + size),
+            cost_estimate=cost(12, width),
+            name=f"part{part}_pairs",
+        )(places, unit, acc, kacc, from_below, from_above)
+
     got_up, got_down, _, _ = lax.optimization_barrier((got_up, got_down, up, down))
+
+    acc, kacc = add_part(0, first, acc, kacc, got_up, got_down)
+    got_up, got_down, acc = lax.optimization_barrier((got_up, got_down, acc))
     sib_up, sib_down = to_sibling(got_up), to_sibling(got_down)
-
-    acc, kacc = pl.pallas_call(
-        functools.partial(near_kernel, first),
-        in_specs=[SMEM, VMEM, VMEM, VMEM] + [ANY] * 4,
-        out_specs=(VMEM, VMEM),
-        out_shape=sums,
-        scratch_shapes=[
-            pltpu.VMEM((4 * first * BLOCK, width), jnp.bfloat16),
-            pltpu.SemaphoreType.DMA((4,)),
-        ],
-        compiler_params=params(16 + first),
-        cost_estimate=cost(12, width),
-        name="near_pairs",
-    )(places, unit, acc, kacc, got_up, sib_up, got_down, sib_down)
-
+    acc, kacc = add_part(1, first, acc, kacc, sib_up, sib_down)
     far_up, far_down, acc = lax.optimization_barrier((far_up, far_down, acc))
     far_sib_up, far_sib_down = to_sibling(far_up), to_sibling(far_down)
+    acc, kacc = add_part(2, second, acc, kacc, far_up, far_down)
+    far_sib_up, far_sib_down, acc = lax.optimization_barrier((far_sib_up, far_sib_down, acc))
     centered, log_density = pl.pallas_call(
-        functools.partial(last_kernel, second),
-        in_specs=[SMEM, VMEM, VMEM, VMEM] + [ANY] * 4,
+        functools.partial(last_kernel, 3),
+        in_specs=[SMEM] + [VMEM] * 5,
         out_specs=(ANY, VMEM),
         out_shape=(
             jax.ShapeDtypeStruct((rows, width), jnp.bfloat16),
@@ -496,14 +495,12 @@
             pltpu.VMEM((BLOCK, width), jnp.float32),
             pltpu.VMEM((BLOCK, BLOCK), jnp.float32),
             pltpu.VMEM((rows, width), jnp.bfloat16),
-            pltpu.VMEM((4 * second * BLOCK, width), jnp.bfloat16),
-            pltpu.SemaphoreType.DMA((4,)),
             pltpu.SemaphoreType.DMA((BPD,)),
         ],
-        compiler_params=params(16 + second),
+        compiler_params=params(14 + second),
         cost_estimate=cost(8, width),
-        name="far_pairs",
-    )(places, unit, acc, kacc, far_up, far_sib_up, far_down, far_sib_down)
+        name="part3_pairs",
+    )(places, unit, acc, kacc, far_sib_up, far_sib_down)
     return centered, log_density
 
 
@@ -521,29 +518,36 @@
         out_specs=pl.BlockSpec((step, width), lambda i: (i, 0)),
         out_shape=jax.ShapeDtypeStruct(embeddings.shape, jnp.bfloat16),
         cost_estimate=pl.CostEstimate(flops=2**22, bytes_accessed=2**22, transcendentals=1024),
+        compiler_params=params(8),
         name="normalize",
     )(embeddings)
 
-    packed = jnp.concatenate([count[:, None], pairs[:, :MOST, 0] * 8 + pairs[:, :MOST, 1]], axis=1)
-    tables = jnp.pad(packed.reshape(1, -1), ((0, 0), (0, 128 - shifts * ENTRY)))
-    for bit in (1, 2, 4):
-        route = [(o, o ^ bit) for o in range(OWNERS)]
-        came = lax.ppermute(tables, "owner", route)
-        if bit == 1:
-            came, unit = lax.optimization_barrier((came, unit))
-            sib = to_sibling(unit)
-        tables = jnp.concatenate([tables, came], axis=0)
-
-    plan, chosen = pl.pallas_call(
+    codes = jnp.sum(pairs * jnp.array([8, 1], jnp.int32), axis=-1)
+    table = jnp.pad(codes, ((0, 8 - shifts), (0, 128 - codes.shape[1]))) + jnp.pad(
+        count[None], ((COUNTS, 7 - COUNTS), (0, 128 - shifts))
+    )
+
+    def turned(x, bits):
+        return lax.ppermute(x, "owner", [(o, o ^ bits) for o in range(OWNERS)])
+
+    came, unit = lax.optimization_barrier((turned(table, 1), unit))
+    sib = to_sibling(unit)
+    tables = jnp.concatenate([table, came], axis=0)
+    tables = [tables] + [turned(tables, bits) for bits in (2, 4, 6)]
+
+    plan, tables, chosen = pl.pallas_call(
         plan_kernel,
-        in_specs=[SMEM, SMEM],
-        out_specs=(SMEM, SMEM),
+        in_specs=[SMEM] + [VMEM] * 4,
+        out_specs=(SMEM, SMEM, SMEM),
         out_shape=(
             jax.ShapeDtypeStruct((PLAN,), jnp.int32),
+            jax.ShapeDtypeStruct((OWNERS * 8, 128), jnp.int32),
             jax.ShapeDtypeStruct((1,), jnp.int32),
         ),
+        scratch_shapes=[pltpu.SemaphoreType.DMA((4,))],
+        compiler_params=params(4),
         name="plan",
-    )(pos, tables)
+    )(pos, *tables)
 
     centered, log_density = lax.switch(
         chosen[0],

time: 77.4 us -> 79.1 us (1.022); the launches traced: 77.7 us -> 77.6 us
  Pallas kernels: 33 us -> 29.3 us
  waiting for transfers between devices: 24.1 us -> 27.1 us
  other arithmetic: 0.11 us -> 1.45 us
    pallas_call x1, Pallas kernels: 4.61 us -> 1.19 us  [shards(): pl.pallas_call(normalize_kernel, grid=(rows // step,), in_specs=[pl.Block...]
    ppermute x4, waiting for transfers between devices: 18.8 us -> 21.7 us  [along_chips(): return lax.ppermute(x, 'owner', route)]
    ppermute x3 -> x4, waiting for transfers between devices: 2.02 us -> 3.34 us  [turned(): return lax.ppermute(x, 'owner', [(o, o ^ bits) for o in range(OWNERS)])]
    ppermute x5, waiting for transfers between devices: 3.3 us -> 2.01 us  [to_sibling(): return lax.ppermute(x, 'owner', [(o, o ^ 1) for o in range(OWNERS)])]
    pallas_call x3 -> x5, Pallas kernels: 14.4 us -> 13.3 us  [the longest x3 4.65 us: add_part(): pl.pallas_call(functools.partial(part_kernel, part), in_specs=[SMEM] + [V...]
    ppermute x3 -> x4, starting transfers between devices: 6.03 us -> 4.99 us  [turned(): return lax.ppermute(x, 'owner', [(o, o ^ bits) for o in range(OWNERS)])]
    unnamed x3 -> x4, local copies, waits for them, and re-layouts: 0.69 us -> 1.59 us
  transfers between devices with their start and end apart: 12 -> 13, of which waited for: 8 -> 6; matrix products, arithmetic and copies ran while one was open for 0% -> 0% of each run, Pallas kernels for 28% -> 23%
where the time goes in v1:
time: 79.1 us; the launch traced here: 77.6 us
  Pallas kernels  29.3 us (37%)
  waiting for transfers between devices  27.1 us (34%)
  starting transfers between devices  14.9 us (19%)
  local copies, waits for them, and re-layouts  3 us (4%)
  between operations  1.52 us (2%)
  other arithmetic  1.45 us (2%)
    ppermute x4, waiting for transfers between devices, along_chips(): return lax.ppermute(x, 'owner', route)  21.7 us
    pallas_call x1, Pallas kernels, exchange_and_score(): pl.pallas_call(own_kernel, in_specs=[SMEM, SMEM, SMEM, VMEM, VMEM], out_s...  8.31 us
    ppermute x4, starting transfers between devices, along_chips(): return lax.ppermute(x, 'owner', route)  5.99 us
    ppermute x4, starting transfers between devices, turned(): return lax.ppermute(x, 'owner', [(o, o ^ bits) for o in range(OWNERS)])  4.99 us
    pallas_call x3, Pallas kernels, add_part(): pl.pallas_call(functools.partial(part_kernel, part), in_specs=[SMEM] + [V...  4.65 us
    pallas_call x1, Pallas kernels, shards(): pl.pallas_call(plan_kernel, in_specs=[SMEM] + [VMEM] * 4, out_specs=(SMEM...  4.51 us
    pallas_call x1, Pallas kernels, exchange_and_score(): pl.pallas_call(functools.partial(last_kernel, 3), in_specs=[SMEM] + [VMEM...  4.11 us
    ppermute x5, starting transfers between devices, to_sibling(): return lax.ppermute(x, 'owner', [(o, o ^ 1) for o in range(OWNERS)])  3.96 us
  transfers between devices with their start and end apart: 13, of which 6 were waited for; matrix products, arithmetic and copies ran while one was open for 0% of the time, Pallas kernels for 23%

profile of v1, /device:TPU:1, one launch (start us, length us, event | category | flops | bytes accessed | tf_op | source)
XLA Modules:
  0.0 77.6 jit_solution(14532288908875728533)
XLA Ops:
  0.6 0.8 fusion
  1.4 0.7 pad_add_fusion.1
  2.1 1.4 %collective-permute-start.24 = (s32[8,128]{1,0:T(8,128)S(1)}, s32[8,128]{1,0:T(8,128)S(1)}, u32[]{:S(2)}, u32[]{:S(2)}) collective-permute-start(s32[8,128]{1,0:T(8,128)S(1)} %pad_add_fusion.1), channel_id=1, source_target_pairs={{0,1},{1,0},{2,3},{3,2},{4,5},{5,4},{6,7},{7,6},{8,9},{9,8},{10,11... | collective-permute-start | bytes 12296 | tf_op jit(solution)/shard_map/ppermute | solution.py:531
  3.5 1.6 %copy-done = bf16[1024,1024]{1,0:T(8,128)(2,1)S(1)} copy-done((bf16[1024,1024]{1,0:T(8,128)(2,1)S(1)}, bf16[1024,1024]{1,0:T(8,128)(2,1)}, u32[]{:S(2)}) %copy-start) | copy-done | bytes 2097176
  5.1 1.2 %normalize.1 = bf16[1024,1024]{1,0:T(8,128)(2,1)S(1)} custom-call(bf16[1024,1024]{1,0:T(8,128)(2,1)S(1)} %copy-done), custom_call_target="tpu_custom_call" | custom-call | flops 4194304 | bytes 4194304 | tf_op jit(solution)/shard_map/normalize/pallas_call | solution.py:514
  6.3 0.1 collective-permute-start.28
  6.4 2.9 %collective-permute-start.27 = (s32[16,128]{1,0:T(8,128)S(1)}, s32[16,128]{1,0:T(8,128)S(1)}, u32[]{:S(2)}, u32[]{:S(2)}) collective-permute-start(s32[16,128]{1,0:T(8,128)S(1)} %pad_add_fusion.t0), channel_id=1, source_target_pairs={{0,6},{1,7},{2,4},{3,5},{4,2},{5,3},{6,0},{7,1},{8,14},{9,15},{10,... | collective-permute-start | bytes 24584 | tf_op jit(solution)/shard_map/ppermute | solution.py:531
  9.3 0.3 collective-permute-start.26
  9.7 0.3 collective-permute-start.25
  10.0 0.4 collective-permute-done.27.t3
  10.3 3.0 %collective-permute-done.26.t2 = s32[16,128]{1,0:T(8,128)S(1)} collective-permute-done((s32[16,128]{1,0:T(8,128)S(1)}, s32[16,128]{1,0:T(8,128)S(1)}, u32[]{:S(2)}, u32[]{:S(2)}) %collective-permute-start.26) | collective-permute-done | bytes 8224 | tf_op jit(solution)/shard_map/ppermute | solution.py:531
  13.3 4.5 %plan.1 = (s32[768]{0:T(1024)S(1)}, s32[64,128]{1,0:T(8,128)S(1)}, s32[1]{0:T(128)}) custom-call(s32[1]{0:T(128)} %bitcast.6.pos_ref, s32[16,128]{1,0:T(8,128)S(1)} %pad_add_fusion.t0, s32[16,128]{1,0:T(8,128)S(1)} %collective-permute-done.25.t1, s32[16,128]{1,0:T(8,128)S(1)} %collective-permute-done.26.t2, s32[16,128]{1,0:T(8,128)S(1)} %collective-permute-done.27.t3), custom_call_target="tpu_custom_call" | custom-call | tf_op jit(solution)/shard_map/plan/pallas_call | solution.py:538
  18.5 58.9 %conditional.1 = (bf16[1024,1024]{1,0:T(8,128)(2,1)}, f32[1024]{0:T(1024)}) conditional(s32[]{:T(128)} %bitcast.9, (s32[1]{0:T(128)}, s32[768]{0:T(1024)S(1)}, bf16[1024,1024]{1,0:T(8,128)(2,1)S(1)}, bf16[1024,1024]{1,0:T(8,128)(2,1)}, s32[1,1,16,3]{2,1,3,0:T(1,128)S(1)}, /*index=5*/s32[64,128]{1,0:T(8,128)S(1)}) %tuple.49, ...), branch_computations={%region_1.2_spmd, %region_2.3_spmd, %region_3.4_spmd} | conditional | flops 8321499136 | bytes 134218896 | solution.py:552
  18.5 1.3 %copy-done.1 = bf16[1024,1024]{1,0:T(8,128)(2,1)} copy-done((bf16[1024,1024]{1,0:T(8,128)(2,1)}, bf16[1024,1024]{1,0:T(8,128)(2,1)S(1)}, u32[]{:S(2)}) %copy-start.1) | copy-done | bytes 2097176 | tf_op jit(solution)/shard_map/cond
  19.8 2.5 %first_pack.3 = (bf16[384,1024]{1,0:T(8,128)(2,1)S(1)}, bf16[384,1024]{1,0:T(8,128)(2,1)S(1)}) custom-call(s32[1]{0:T(128)} %get-tuple-element.46.pos_ref, s32[768]{0:T(1024)S(1)} %get-tuple-element.47.plan_ref, bf16[1024,1024]{1,0:T(8,128)(2,1)} %copy-done.1, bf16[1024,1024]{1,0:T(8,128)(2,1)} %get-tuple-element.49.sib_ref), custom_call_target="tpu_custom_call" | custom-call | tf_op jit(solution)/shard_map/cond/branch_0_fun/first_pack/pallas_call | solution.py:422
  22.4 2.7 %collective-permute-start.1 = (bf16[384,1024]{1,0:T(8,128)(2,1)S(1)}, bf16[384,1024]{1,0:T(8,128)(2,1)S(1)}, u32[]{:S(2)}, u32[]{:S(2)}) collective-permute-start(bf16[384,1024]{1,0:T(8,128)(2,1)S(1)} %get-tuple-element.51), channel_id=1, source_target_pairs={{0,6},{1,7},{2,0},{3,1},{4,2},{5,3},{6,4},{7,5},{8,14},{9,15},{10,... | collective-permute-start | bytes 2359304 | tf_op jit(solution)/shard_map/cond/branch_0_fun/ppermute | solution.py:39
  25.1 0.1 copy.13.surplus_ref
  25.2 2.1 %places.3.task_ref = s32[1152]{0:T(1024)S(1)} custom-call(s32[1]{0:T(128)} %get-tuple-element.46.pos_ref, s32[64,128]{1,0:T(8,128)S(1)} %get-tuple-element.52.tab_ref, s32[768]{0:T(1024)S(1)} %get-tuple-element.47.plan_ref), custom_call_target="tpu_custom_call" | custom-call | flops 1073741824 | bytes 8388608 | tf_op jit(solution)/shard_map/cond/branch_0_fun/places/pallas_call | solution.py:433
  27.3 8.3 %own_pairs.3 = (f32[1024,1024]{1,0:T(8,128)S(1)}, f32[1024,128]{1,0:T(8,128)S(1)}) custom-call(s32[1]{0:T(128)} %get-tuple-element.46.pos_ref, s32[64,128]{1,0:T(8,128)S(1)} %get-tuple-element.52.tab_ref, s32[16,3]{1,0:T(8,128)S(1)} %copy.13.surplus_ref, bf16[1024,1024]{1,0:T(8,128)(2,1)S(1)} %copy-done.2, bf16[1024,1024]{1,0:T(8,128)(2,1)} %get-tuple-element.49.sib_ref), custom_call_target="tpu_custom_call" | custom-call | flops 4294967296 | bytes 8388608 | tf_op jit(solution)/shard_map/cond/branch_0_fun/own_pairs/pallas_call | solution.py:442
  35.6 5.2 %collective-permute-done.got_up.up_ref = bf16[384,1024]{1,0:T(8,128)(2,1)S(1)} collective-permute-done((bf16[384,1024]{1,0:T(8,128)(2,1)S(1)}, bf16[384,1024]{1,0:T(8,128)(2,1)S(1)}, u32[]{:S(2)}, u32[]{:S(2)}) %collective-permute-start) | collective-permute-done | bytes 786464 | tf_op jit(solution)/shard_map/cond/branch_0_fun/ppermute | solution.py:39
  40.8 1.9 %second_pack.3 = (bf16[384,1024]{1,0:T(8,128)(2,1)S(1)}, bf16[384,1024]{1,0:T(8,128)(2,1)S(1)}) custom-call(s32[1]{0:T(128)} %get-tuple-element.46.pos_ref, s32[768]{0:T(1024)S(1)} %get-tuple-element.47.plan_ref, bf16[1024,1024]{1,0:T(8,128)(2,1)S(1)} %copy-done.2, bf16[1024,1024]{1,0:T(8,128)(2,1)} %get-tuple-element.49.sib_ref, ...), custom_call_target="tpu_custom_call" | custom-call | tf_op jit(solution)/shard_map/cond/branch_0_fun/second_pack/pallas_call | solution.py:454
  42.8 2.6 %part0_pairs.3 = (f32[1024,1024]{1,0:T(8,128)S(1)}, f32[1024,128]{1,0:T(8,128)S(1)}) custom-call(s32[1152]{0:T(1024)S(1)} %places.3.task_ref, bf16[1024,1024]{1,0:T(8,128)(2,1)S(1)} %copy-done.2, f32[1024,1024]{1,0:T(8,128)S(1)} %get-tuple-element.62.acc_in, f32[1024,128]{1,0:T(8,128)S(1)} %get-tuple-element.63.kacc_in, ...), custom_call_target="tpu_custom_call" | custom-call | flops 805306368 | bytes 8388608 | tf_op jit(solution)/shard_map/cond/branch_0_fun/part0_pairs/pallas_call | solution.py:466
  45.4 2.8 %collective-permute-start.4 = (bf16[384,1024]{1,0:T(8,128)(2,1)S(1)}, bf16[384,1024]{1,0:T(8,128)(2,1)S(1)}, u32[]{:S(2)}, u32[]{:S(2)}) collective-permute-start(bf16[384,1024]{1,0:T(8,128)(2,1)S(1)} %collective-permute-done.got_up.up_ref), channel_id=1, source_target_pairs={{0,1},{1,0},{2,3},{3,2},{4,5},{5,4},{6,7},{7,6},{8,9},{9,8},{10,11... | collective-permute-start | bytes 2359304 | tf_op jit(solution)/shard_map/cond/branch_0_fun/ppermute | solution.py:43
  48.2 0.1 collective-permute-start.5
  48.3 3.2 %collective-permute-start.3 = (bf16[384,1024]{1,0:T(8,128)(2,1)S(1)}, bf16[384,1024]{1,0:T(8,128)(2,1)S(1)}, u32[]{:S(2)}, u32[]{:S(2)}) collective-permute-start(bf16[384,1024]{1,0:T(8,128)(2,1)S(1)} %get-tuple-element.59), channel_id=1, source_target_pairs={{0,6},{1,7},{2,0},{3,1},{4,2},{5,3},{6,4},{7,5},{8,14},{9,15},{10,... | collective-permute-start | bytes 2359304 | tf_op jit(solution)/shard_map/cond/branch_0_fun/ppermute | solution.py:39
  51.6 1.0 %part1_pairs.3 = (f32[1024,1024]{1,0:T(8,128)S(1)}, f32[1024,128]{1,0:T(8,128)S(1)}) custom-call(s32[1152]{0:T(1024)S(1)} %places.3.task_ref, bf16[1024,1024]{1,0:T(8,128)(2,1)S(1)} %copy-done.2, f32[1024,1024]{1,0:T(8,128)S(1)} %get-tuple-element.65.acc_in, f32[1024,128]{1,0:T(8,128)S(1)} %get-tuple-element.66.kacc_in, ...), custom_call_target="tpu_custom_call" | custom-call | flops 805306368 | bytes 8388608 | tf_op jit(solution)/shard_map/cond/branch_0_fun/part1_pairs/pallas_call | solution.py:466
  52.6 16.5 %collective-permute-done.2.up_ref = bf16[384,1024]{1,0:T(8,128)(2,1)S(1)} collective-permute-done((bf16[384,1024]{1,0:T(8,128)(2,1)S(1)}, bf16[384,1024]{1,0:T(8,128)(2,1)S(1)}, u32[]{:S(2)}, u32[]{:S(2)}) %collective-permute-start.2) | collective-permute-done | bytes 786464 | tf_op jit(solution)/shard_map/cond/branch_0_fun/ppermute | solution.py:39
  69.1 0.9 %collective-permute-start.6 = (bf16[384,1024]{1,0:T(8,128)(2,1)S(1)}, bf16[384,1024]{1,0:T(8,128)(2,1)S(1)}, u32[]{:S(2)}, u32[]{:S(2)}) collective-permute-start(bf16[384,1024]{1,0:T(8,128)(2,1)S(1)} %collective-permute-done.2.up_ref), channel_id=1, source_target_pairs={{0,1},{1,0},{2,3},{3,2},{4,5},{5,4},{6,7},{7,6},{8,9},{9,8},{10,11... | collective-permute-start | bytes 2359304 | tf_op jit(solution)/shard_map/cond/branch_0_fun/ppermute | solution.py:43
  70.0 1.0 %part2_pairs.3 = (f32[1024,1024]{1,0:T(8,128)S(1)}, f32[1024,128]{1,0:T(8,128)S(1)}) custom-call(s32[1152]{0:T(1024)S(1)} %places.3.task_ref, bf16[1024,1024]{1,0:T(8,128)(2,1)S(1)} %copy-done.2, f32[1024,1024]{1,0:T(8,128)S(1)} %get-tuple-element.72.acc_in, f32[1024,128]{1,0:T(8,128)S(1)} %get-tuple-element.73.kacc_in, ...), custom_call_target="tpu_custom_call" | custom-call | flops 805306368 | bytes 8388608 | tf_op jit(solution)/shard_map/cond/branch_0_fun/part2_pairs/pallas_call | solution.py:466
  71.1 0.9 %collective-permute-done.6.up_ref = bf16[384,1024]{1,0:T(8,128)(2,1)S(1)} collective-permute-done((bf16[384,1024]{1,0:T(8,128)(2,1)S(1)}, bf16[384,1024]{1,0:T(8,128)(2,1)S(1)}, u32[]{:S(2)}, u32[]{:S(2)}) %collective-permute-start.6) | collective-permute-done | bytes 786464 | tf_op jit(solution)/shard_map/cond/branch_0_fun/ppermute | solution.py:43
  72.0 1.1 %collective-permute-done.7.down_ref = bf16[384,1024]{1,0:T(8,128)(2,1)S(1)} collective-permute-done((bf16[384,1024]{1,0:T(8,128)(2,1)S(1)}, bf16[384,1024]{1,0:T(8,128)(2,1)S(1)}, u32[]{:S(2)}, u32[]{:S(2)}) %collective-permute-start.7) | collective-permute-done | bytes 786464 | tf_op jit(solution)/shard_map/cond/branch_0_fun/ppermute | solution.py:43
  73.1 4.1 %part3_pairs.3 = (bf16[1024,1024]{1,0:T(8,128)(2,1)}, f32[8,128]{1,0:T(8,128)}) custom-call(s32[1152]{0:T(1024)S(1)} %places.3.task_ref, bf16[1024,1024]{1,0:T(8,128)(2,1)S(1)} %copy-done.2, f32[1024,1024]{1,0:T(8,128)S(1)} %get-tuple-element.75.acc_in, f32[1024,128]{1,0:T(8,128)S(1)} %get-tuple-element.76.kacc_in, ...), custom_call_target="tpu_custom_call" | custom-call | flops 536870912 | bytes 8388608 | tf_op jit(solution)/shard_map/cond/branch_0_fun/part3_pairs/pallas_call | solution.py:486
  (18 shorter events, 0.1 us)
Async XLA Ops:
  2.1 4.2 %collective-permute-start.24 = (s32[8,128]{1,0:T(8,128)S(1)}, s32[8,128]{1,0:T(8,128)S(1)}, u32[]{:S(2)}, u32[]{:S(2)}) collective-permute-start(s32[8,128]{1,0:T(8,128)S(1)} %pad_add_fusion.1), channel_id=1, source_target_pairs={{0,1},{1,0},{2,3},{3,2},{4,5},{5,4},{6,7},{7,6},{8,9},{9,8},{10,11... | collective-permute-start | bytes 12296 | tf_op jit(solution)/shard_map/ppermute | solution.py:531
  3.5 1.6 %copy-start = (bf16[1024,1024]{1,0:T(8,128)(2,1)S(1)}, bf16[1024,1024]{1,0:T(8,128)(2,1)}, u32[]{:S(2)}) copy-start(bf16[1024,1024]{1,0:T(8,128)(2,1)} %x_ref.1) | copy-start | bytes 6291460
  5.1 13.4 %copy-start.7 = (s32[1,1,16,3]{2,1,3,0:T(1,128)S(1)}, s32[1,1,16,3]{2,1,3,0:T(1,128)}, u32[]{:S(2)}) copy-start(s32[1,1,16,3]{2,1,3,0:T(1,128)} %param.11) | copy-start | bytes 580
  6.3 12.2 %collective-permute-start.28 = (bf16[1024,1024]{1,0:T(8,128)(2,1)S(1)}, bf16[1024,1024]{1,0:T(8,128)(2,1)}, u32[]{:S(2)}, u32[]{:S(2)}) collective-permute-start(bf16[1024,1024]{1,0:T(8,128)(2,1)S(1)} %normalize.1), channel_id=1, source_target_pairs={{0,1},{1,0},{2,3},{3,2},{4,5},{5,4},{6,7},{7,6},{8,9},{9,8},{10,11... | collective-permute-start | bytes 6291464 | tf_op jit(solution)/shard_map/ppermute | solution.py:43
  6.4 3.9 %collective-permute-start.27 = (s32[16,128]{1,0:T(8,128)S(1)}, s32[16,128]{1,0:T(8,128)S(1)}, u32[]{:S(2)}, u32[]{:S(2)}) collective-permute-start(s32[16,128]{1,0:T(8,128)S(1)} %pad_add_fusion.t0), channel_id=1, source_target_pairs={{0,6},{1,7},{2,4},{3,5},{4,2},{5,3},{6,0},{7,1},{8,14},{9,15},{10,... | collective-permute-start | bytes 24584 | tf_op jit(solution)/shard_map/ppermute | solution.py:531
  9.3 4.0 %collective-permute-start.26 = (s32[16,128]{1,0:T(8,128)S(1)}, s32[16,128]{1,0:T(8,128)S(1)}, u32[]{:S(2)}, u32[]{:S(2)}) collective-permute-start(s32[16,128]{1,0:T(8,128)S(1)} %pad_add_fusion.t0), channel_id=1, source_target_pairs={{0,4},{1,5},{2,6},{3,7},{4,0},{5,1},{6,2},{7,3},{8,12},{9,13},{10,... | collective-permute-start | bytes 24584 | tf_op jit(solution)/shard_map/ppermute | solution.py:531
  9.7 3.7 %collective-permute-start.25 = (s32[16,128]{1,0:T(8,128)S(1)}, s32[16,128]{1,0:T(8,128)S(1)}, u32[]{:S(2)}, u32[]{:S(2)}) collective-permute-start(s32[16,128]{1,0:T(8,128)S(1)} %pad_add_fusion.t0), channel_id=1, source_target_pairs={{0,2},{1,3},{2,0},{3,1},{4,6},{5,7},{6,4},{7,5},{8,10},{9,11},{10,... | collective-permute-start | bytes 24584 | tf_op jit(solution)/shard_map/ppermute | solution.py:531
  18.5 1.3 %copy-start.1 = (bf16[1024,1024]{1,0:T(8,128)(2,1)}, bf16[1024,1024]{1,0:T(8,128)(2,1)S(1)}, u32[]{:S(2)}) copy-start(bf16[1024,1024]{1,0:T(8,128)(2,1)S(1)} %get-tuple-element.48.unit_ref.u_ref) | copy-start | bytes 6291460 | tf_op jit(solution)/shard_map/cond
  22.4 18.5 %collective-permute-start = (bf16[384,1024]{1,0:T(8,128)(2,1)S(1)}, bf16[384,1024]{1,0:T(8,128)(2,1)S(1)}, u32[]{:S(2)}, u32[]{:S(2)}) collective-permute-start(bf16[384,1024]{1,0:T(8,128)(2,1)S(1)} %get-tuple-element.50), channel_id=1, source_target_pairs={{0,2},{1,3},{2,4},{3,5},{4,6},{5,7},{6,0},{7,1},{8,10},{9,11},{10,... | collective-permute-start | bytes 2359304 | tf_op jit(solution)/shard_map/cond/branch_0_fun/ppermute | solution.py:39
  22.4 18.4 %collective-permute-start.1 = (bf16[384,1024]{1,0:T(8,128)(2,1)S(1)}, bf16[384,1024]{1,0:T(8,128)(2,1)S(1)}, u32[]{:S(2)}, u32[]{:S(2)}) collective-permute-start(bf16[384,1024]{1,0:T(8,128)(2,1)S(1)} %get-tuple-element.51), channel_id=1, source_target_pairs={{0,6},{1,7},{2,0},{3,1},{4,2},{5,3},{6,4},{7,5},{8,14},{9,15},{10,... | collective-permute-start | bytes 2359304 | tf_op jit(solution)/shard_map/cond/branch_0_fun/ppermute | solution.py:39
  25.2 2.1 %copy-start.2 = (bf16[1024,1024]{1,0:T(8,128)(2,1)S(1)}, bf16[1024,1024]{1,0:T(8,128)(2,1)}, u32[]{:S(2)}) copy-start(bf16[1024,1024]{1,0:T(8,128)(2,1)} %copy-done.1) | copy-start | bytes 6291460 | tf_op jit(solution)/shard_map/cond
  45.4 6.2 %collective-permute-start.4 = (bf16[384,1024]{1,0:T(8,128)(2,1)S(1)}, bf16[384,1024]{1,0:T(8,128)(2,1)S(1)}, u32[]{:S(2)}, u32[]{:S(2)}) collective-permute-start(bf16[384,1024]{1,0:T(8,128)(2,1)S(1)} %collective-permute-done.got_up.up_ref), channel_id=1, source_target_pairs={{0,1},{1,0},{2,3},{3,2},{4,5},{5,4},{6,7},{7,6},{8,9},{9,8},{10,11... | collective-permute-start | bytes 2359304 | tf_op jit(solution)/shard_map/cond/branch_0_fun/ppermute | solution.py:43
  48.2 3.4 %collective-permute-start.5 = (bf16[384,1024]{1,0:T(8,128)(2,1)S(1)}, bf16[384,1024]{1,0:T(8,128)(2,1)S(1)}, u32[]{:S(2)}, u32[]{:S(2)}) collective-permute-start(bf16[384,1024]{1,0:T(8,128)(2,1)S(1)} %collective-permute-done.1.got_down.down_ref), channel_id=1, source_target_pairs={{0,1},{1,0},{2,3},{3,2},{4,5},{5,4},{6,7},{7,6},{8,9},{9,8},{10,11... | collective-permute-start | bytes 2359304 | tf_op jit(solution)/shard_map/cond/branch_0_fun/ppermute | solution.py:43
  48.3 20.8 %collective-permute-start.2 = (bf16[384,1024]{1,0:T(8,128)(2,1)S(1)}, bf16[384,1024]{1,0:T(8,128)(2,1)S(1)}, u32[]{:S(2)}, u32[]{:S(2)}) collective-permute-start(bf16[384,1024]{1,0:T(8,128)(2,1)S(1)} %get-tuple-element.58), channel_id=1, source_target_pairs={{0,2},{1,3},{2,4},{3,5},{4,6},{5,7},{6,0},{7,1},{8,10},{9,11},{10,... | collective-permute-start | bytes 2359304 | tf_op jit(solution)/shard_map/cond/branch_0_fun/ppermute | solution.py:39
  48.3 20.8 %collective-permute-start.3 = (bf16[384,1024]{1,0:T(8,128)(2,1)S(1)}, bf16[384,1024]{1,0:T(8,128)(2,1)S(1)}, u32[]{:S(2)}, u32[]{:S(2)}) collective-permute-start(bf16[384,1024]{1,0:T(8,128)(2,1)S(1)} %get-tuple-element.59), channel_id=1, source_target_pairs={{0,6},{1,7},{2,0},{3,1},{4,2},{5,3},{6,4},{7,5},{8,14},{9,15},{10,... | collective-permute-start | bytes 2359304 | tf_op jit(solution)/shard_map/cond/branch_0_fun/ppermute | solution.py:39
  69.1 2.8 %collective-permute-start.6 = (bf16[384,1024]{1,0:T(8,128)(2,1)S(1)}, bf16[384,1024]{1,0:T(8,128)(2,1)S(1)}, u32[]{:S(2)}, u32[]{:S(2)}) collective-permute-start(bf16[384,1024]{1,0:T(8,128)(2,1)S(1)} %collective-permute-done.2.up_ref), channel_id=1, source_target_pairs={{0,1},{1,0},{2,3},{3,2},{4,5},{5,4},{6,7},{7,6},{8,9},{9,8},{10,11... | collective-permute-start | bytes 2359304 | tf_op jit(solution)/shard_map/cond/branch_0_fun/ppermute | solution.py:43
  70.0 3.0 %collective-permute-start.7 = (bf16[384,1024]{1,0:T(8,128)(2,1)S(1)}, bf16[384,1024]{1,0:T(8,128)(2,1)S(1)}, u32[]{:S(2)}, u32[]{:S(2)}) collective-permute-start(bf16[384,1024]{1,0:T(8,128)(2,1)S(1)} %collective-permute-done.3.down_ref), channel_id=1, source_target_pairs={{0,1},{1,0},{2,3},{3,2},{4,5},{5,4},{6,7},{7,6},{8,9},{9,8},{10,11... | collective-permute-start | bytes 2359304 | tf_op jit(solution)/shard_map/cond/branch_0_fun/ppermute | solution.py:43
